TPU v7x, 32 devices: a whole 2x2x4 slice. The times are simulated.
32 devices in a mesh: blk: 8 (over y, x, core), grp: 4 (over z).
Axes of the slice: x: 2, y: 2, z: 4, core: 2. Of those that a mesh axis runs over, the one named last changes fastest.
Arguments:
- picture_embedding_array: bfloat16 [8192, 1152], P(('blk', 'grp')), may hold values from -0.1875 to 0.1875
- caption_embedding_array: bfloat16 [8192, 1152], P(('blk', 'grp')), may hold values from -0.1875 to 0.1875
- sharpness_multiplier: float32 [1], replicated, may hold values from 8 to 16
- score_offset: float32 [1], replicated, may hold values from -6 to -3
Outputs:
- row_loss: float32 [8192], P(('blk', 'grp'))
- grad_images: float32 [8192, 1152], P(('blk', 'grp'))
- grad_texts: float32 [8192, 1152], P(('blk', 'grp'))
All inputs are finite; a program needn't handle non-finite values.
Results may differ from a plain program's by a relative error of at most 0.02.
Values may be sent and summed in bfloat16 or wider, within the bound.
A program may use at most 64 MiB of HBM per device.

v0:
```python
import jax
import jax.numpy as jnp
from jax import lax
from jax.sharding import PartitionSpec as P

KSTEPS = 8


def passed_along(block, axis, distance):
    devices = range(lax.axis_size(axis))
    route = [((i - distance) % len(devices), i) for i in devices]
    return lax.ppermute(block, axis, route)


def normalize(raw):
    computed_quantities = raw.astype(jnp.float32)
    inverse = lax.rsqrt(
        jnp.sum(computed_quantities * computed_quantities, axis=-1, keepdims=True) + 1e-06
    )
    return (computed_quantities * inverse, inverse)


def back_norm(unit32, inverse, grad_unit):
    along = jnp.sum(unit32 * grad_unit, axis=-1, keepdims=True)
    return inverse * (grad_unit - unit32 * along)


def pairwise_loss_terms(
    image_block_rows, text_block_rows, target_labels, smoothing_coefficient, block_displacement
):
    pair_logit_matrix = (
        smoothing_coefficient
        * lax.dot_general(
            image_block_rows,
            text_block_rows,
            (((1,), (1,)), ((), ())),
            preferred_element_type=jnp.float32,
        )
        + block_displacement
    )
    row_portion = jnp.sum(jax.nn.softplus(-target_labels * pair_logit_matrix), axis=-1)
    sigmoid_weights = (
        -target_labels * jax.nn.sigmoid(-target_labels * pair_logit_matrix) * smoothing_coefficient
    ).astype(jnp.bfloat16)
    return (row_portion, sigmoid_weights)


def image_side(sigmoid_weights, text_block_rows):
    return jnp.dot(sigmoid_weights, text_block_rows, preferred_element_type=jnp.float32)


def text_side(sigmoid_weights, image_block_rows):
    return lax.dot_general(
        sigmoid_weights,
        image_block_rows,
        (((0,), (0,)), ((), ())),
        preferred_element_type=jnp.float32,
    )


def on_device(picture_embedding_array, caption_embedding_array, sharpness_multiplier, score_offset):
    smoothing_coefficient = sharpness_multiplier[0]
    block_displacement = score_offset[0]
    rows = picture_embedding_array.shape[0]
    img_unit32, img_inverse = normalize(picture_embedding_array)
    txt_unit32, txt_inverse = normalize(caption_embedding_array)
    image_unit_vectors = img_unit32.astype(jnp.bfloat16)
    text_unit_vectors = txt_unit32.astype(jnp.bfloat16)
    positions = lax.broadcasted_iota(jnp.int32, (rows, rows), 0)
    columns = lax.broadcasted_iota(jnp.int32, (rows, rows), 1)
    initial_label_values = jnp.where(positions == columns, 1.0, -1.0).astype(jnp.float32)
    negative_labels = jnp.full((rows, rows), -1.0, jnp.float32)
    row_total_sum, sigmoid_weights = pairwise_loss_terms(
        image_unit_vectors,
        text_unit_vectors,
        initial_label_values,
        smoothing_coefficient,
        block_displacement,
    )
    grad_img = image_side(sigmoid_weights, text_unit_vectors)
    own_text = text_side(sigmoid_weights, image_unit_vectors)
    incoming_caption_groups = text_unit_vectors
    carried = own_text
    for hop_index in range(1, KSTEPS):
        incoming_caption_groups, carried = (
            passed_along(incoming_caption_groups, ("blk", "grp"), 1),
            passed_along(carried.astype(jnp.bfloat16), ("blk", "grp"), 1).astype(carried.dtype),
        )
        row_portion, sigmoid_weights = pairwise_loss_terms(
            image_unit_vectors,
            incoming_caption_groups,
            negative_labels,
            smoothing_coefficient,
            block_displacement,
        )
        row_total_sum = row_total_sum + row_portion
        grad_img = grad_img + image_side(sigmoid_weights, incoming_caption_groups)
        carried = carried + text_side(sigmoid_weights, image_unit_vectors)
    grad_txt = passed_along(carried.astype(jnp.bfloat16), ("blk", "grp"), 1 - KSTEPS).astype(
        carried.dtype
    )
    grad_images = back_norm(img_unit32, img_inverse, grad_img)
    grad_texts = back_norm(txt_unit32, txt_inverse, grad_txt)
    return (row_total_sum, grad_images, grad_texts)


def solution(mesh):
    return jax.shard_map(
        on_device,
        mesh=mesh,
        in_specs=(P(("blk", "grp"), None), P(("blk", "grp"), None), P(), P()),
        out_specs=(P(("blk", "grp")), P(("blk", "grp"), None), P(("blk", "grp"), None)),
        check_vma=False,
    )
```

profile of v0, /device:TPU:1, one launch (start us, length us, event | category | flops | bytes accessed | tf_op | source)
XLA Modules:
  0.0 205.9 jit_solution(6766295621561198469)
XLA Ops:
  0.6 1.3 fusion.9
  2.0 1.2 fusion.1
  3.2 2.2 %collective-permute-start = (bf16[256,1152]{1,0:T(8,128)(2,1)S(1)}, bf16[256,1152]{1,0:T(8,128)(2,1)S(1)}, u32[]{:S(2)}, u32[]{:S(2)}) collective-permute-start(bf16[256,1152]{1,0:T(8,128)(2,1)S(1)} %fusion.1), channel_id=1, source_target_pairs={{31,0},{0,1},{1,2},{2,3},{3,4},{4,5},{5,6},{6,7},{7,8},{8,9},{9,10... | collective-permute-start | bytes 1769480 | tf_op jit(solution)/shard_map/ppermute | solution.py:12
  6.9 0.6 fusion.21
  7.5 0.5 convolution_convert_fusion
  8.0 1.4 collective-permute-start.7
  9.8 11.9 %collective-permute-done = bf16[256,1152]{1,0:T(8,128)(2,1)S(1)} collective-permute-done((bf16[256,1152]{1,0:T(8,128)(2,1)S(1)}, bf16[256,1152]{1,0:T(8,128)(2,1)S(1)}, u32[]{:S(2)}, u32[]{:S(2)}) %collective-permute-start) | collective-permute-done | bytes 589856 | tf_op jit(solution)/shard_map/ppermute | solution.py:12
  21.6 0.6 fusion.22
  22.2 12.1 %collective-permute-done.7 = bf16[256,1152]{1,0:T(8,128)(2,1)S(1)} collective-permute-done((bf16[256,1152]{1,0:T(8,128)(2,1)S(1)}, bf16[256,1152]{1,0:T(8,128)(2,1)S(1)}, u32[]{:S(2)}, u32[]{:S(2)}) %collective-permute-start.7) | collective-permute-done | bytes 589856 | tf_op jit(solution)/shard_map/ppermute | solution.py:12
  35.2 11.7 %collective-permute-done.1 = bf16[256,1152]{1,0:T(8,128)(2,1)S(1)} collective-permute-done((bf16[256,1152]{1,0:T(8,128)(2,1)S(1)}, bf16[256,1152]{1,0:T(8,128)(2,1)S(1)}, u32[]{:S(2)}, u32[]{:S(2)}) %collective-permute-start.1) | collective-permute-done | bytes 589856 | tf_op jit(solution)/shard_map/ppermute | solution.py:12
  46.9 0.6 fusion.23
  48.0 11.6 %collective-permute-done.8 = bf16[256,1152]{1,0:T(8,128)(2,1)S(1)} collective-permute-done((bf16[256,1152]{1,0:T(8,128)(2,1)S(1)}, bf16[256,1152]{1,0:T(8,128)(2,1)S(1)}, u32[]{:S(2)}, u32[]{:S(2)}) %collective-permute-start.8) | collective-permute-done | bytes 589856 | tf_op jit(solution)/shard_map/ppermute | solution.py:12
  60.2 12.0 %collective-permute-done.2 = bf16[256,1152]{1,0:T(8,128)(2,1)S(1)} collective-permute-done((bf16[256,1152]{1,0:T(8,128)(2,1)S(1)}, bf16[256,1152]{1,0:T(8,128)(2,1)S(1)}, u32[]{:S(2)}, u32[]{:S(2)}) %collective-permute-start.2) | collective-permute-done | bytes 589856 | tf_op jit(solution)/shard_map/ppermute | solution.py:12
  72.2 0.6 fusion.24
  73.2 11.6 %collective-permute-done.9 = bf16[256,1152]{1,0:T(8,128)(2,1)S(1)} collective-permute-done((bf16[256,1152]{1,0:T(8,128)(2,1)S(1)}, bf16[256,1152]{1,0:T(8,128)(2,1)S(1)}, u32[]{:S(2)}, u32[]{:S(2)}) %collective-permute-start.9) | collective-permute-done | bytes 589856 | tf_op jit(solution)/shard_map/ppermute | solution.py:12
  85.4 12.0 %collective-permute-done.3 = bf16[256,1152]{1,0:T(8,128)(2,1)S(1)} collective-permute-done((bf16[256,1152]{1,0:T(8,128)(2,1)S(1)}, bf16[256,1152]{1,0:T(8,128)(2,1)S(1)}, u32[]{:S(2)}, u32[]{:S(2)}) %collective-permute-start.3) | collective-permute-done | bytes 589856 | tf_op jit(solution)/shard_map/ppermute | solution.py:12
  97.5 0.6 fusion.25
  98.5 11.6 %collective-permute-done.10 = bf16[256,1152]{1,0:T(8,128)(2,1)S(1)} collective-permute-done((bf16[256,1152]{1,0:T(8,128)(2,1)S(1)}, bf16[256,1152]{1,0:T(8,128)(2,1)S(1)}, u32[]{:S(2)}, u32[]{:S(2)}) %collective-permute-start.10) | collective-permute-done | bytes 589856 | tf_op jit(solution)/shard_map/ppermute | solution.py:12
  110.7 12.0 %collective-permute-done.4 = bf16[256,1152]{1,0:T(8,128)(2,1)S(1)} collective-permute-done((bf16[256,1152]{1,0:T(8,128)(2,1)S(1)}, bf16[256,1152]{1,0:T(8,128)(2,1)S(1)}, u32[]{:S(2)}, u32[]{:S(2)}) %collective-permute-start.4) | collective-permute-done | bytes 589856 | tf_op jit(solution)/shard_map/ppermute | solution.py:12
  122.8 0.6 fusion.26
  123.8 11.6 %collective-permute-done.11 = bf16[256,1152]{1,0:T(8,128)(2,1)S(1)} collective-permute-done((bf16[256,1152]{1,0:T(8,128)(2,1)S(1)}, bf16[256,1152]{1,0:T(8,128)(2,1)S(1)}, u32[]{:S(2)}, u32[]{:S(2)}) %collective-permute-start.11) | collective-permute-done | bytes 589856 | tf_op jit(solution)/shard_map/ppermute | solution.py:12
  136.0 12.0 %collective-permute-done.5 = bf16[256,1152]{1,0:T(8,128)(2,1)S(1)} collective-permute-done((bf16[256,1152]{1,0:T(8,128)(2,1)S(1)}, bf16[256,1152]{1,0:T(8,128)(2,1)S(1)}, u32[]{:S(2)}, u32[]{:S(2)}) %collective-permute-start.5) | collective-permute-done | bytes 589856 | tf_op jit(solution)/shard_map/ppermute | solution.py:12
  148.0 0.6 fusion.27
  149.1 11.6 %collective-permute-done.12 = bf16[256,1152]{1,0:T(8,128)(2,1)S(1)} collective-permute-done((bf16[256,1152]{1,0:T(8,128)(2,1)S(1)}, bf16[256,1152]{1,0:T(8,128)(2,1)S(1)}, u32[]{:S(2)}, u32[]{:S(2)}) %collective-permute-start.12) | collective-permute-done | bytes 589856 | tf_op jit(solution)/shard_map/ppermute | solution.py:12
  161.5 11.9 %collective-permute-done.6 = bf16[256,1152]{1,0:T(8,128)(2,1)S(1)} collective-permute-done((bf16[256,1152]{1,0:T(8,128)(2,1)S(1)}, bf16[256,1152]{1,0:T(8,128)(2,1)S(1)}, u32[]{:S(2)}, u32[]{:S(2)}) %collective-permute-start.6) | collective-permute-done | bytes 589856 | tf_op jit(solution)/shard_map/ppermute | solution.py:12
  173.3 0.6 fusion.28
  174.4 11.6 %collective-permute-done.13 = bf16[256,1152]{1,0:T(8,128)(2,1)S(1)} collective-permute-done((bf16[256,1152]{1,0:T(8,128)(2,1)S(1)}, bf16[256,1152]{1,0:T(8,128)(2,1)S(1)}, u32[]{:S(2)}, u32[]{:S(2)}) %collective-permute-start.13) | collective-permute-done | bytes 589856 | tf_op jit(solution)/shard_map/ppermute | solution.py:12
  186.1 0.5 fusion.5
  186.6 0.6 add_add_fusion
  187.2 1.3 fusion.7
  188.5 15.7 %collective-permute-done.14 = bf16[256,1152]{1,0:T(8,128)(2,1)S(1)} collective-permute-done((bf16[256,1152]{1,0:T(8,128)(2,1)S(1)}, bf16[256,1152]{1,0:T(8,128)(2,1)S(1)}, u32[]{:S(2)}, u32[]{:S(2)}) %collective-permute-start.14) | collective-permute-done | bytes 589856 | tf_op jit(solution)/shard_map/ppermute | solution.py:12
  204.6 1.3 fusion.11
  (41 shorter events, 7.8 us)
Async XLA Ops:
  0.6 5.4 %copy-start = (bf16[256,1152]{1,0:T(8,128)(2,1)S(1)}, bf16[256,1152]{1,0:T(8,128)(2,1)}, u32[]{:S(2)}) copy-start(bf16[256,1152]{1,0:T(8,128)(2,1)} %param.4) | copy-start | bytes 1769476
  3.2 18.4 %collective-permute-start = (bf16[256,1152]{1,0:T(8,128)(2,1)S(1)}, bf16[256,1152]{1,0:T(8,128)(2,1)S(1)}, u32[]{:S(2)}, u32[]{:S(2)}) collective-permute-start(bf16[256,1152]{1,0:T(8,128)(2,1)S(1)} %fusion.1), channel_id=1, source_target_pairs={{31,0},{0,1},{1,2},{2,3},{3,4},{4,5},{5,6},{6,7},{7,8},{8,9},{9,10... | collective-permute-start | bytes 1769480 | tf_op jit(solution)/shard_map/ppermute | solution.py:12
  8.0 26.3 %collective-permute-start.7 = (bf16[256,1152]{1,0:T(8,128)(2,1)S(1)}, bf16[256,1152]{1,0:T(8,128)(2,1)S(1)}, u32[]{:S(2)}, u32[]{:S(2)}) collective-permute-start(bf16[256,1152]{1,0:T(8,128)(2,1)S(1)} %convolution_convert_fusion), channel_id=1, source_target_pairs={{31,0},{0,1},{1,2},{2,3},{3,4},{4,5},{5,6},{6,7},{7,8},{8,9},{9,10... | collective-permute-start | bytes 1769480 | tf_op jit(solution)/shard_map/ppermute | solution.py:12
  21.6 25.3 %collective-permute-start.1 = (bf16[256,1152]{1,0:T(8,128)(2,1)S(1)}, bf16[256,1152]{1,0:T(8,128)(2,1)S(1)}, u32[]{:S(2)}, u32[]{:S(2)}) collective-permute-start(bf16[256,1152]{1,0:T(8,128)(2,1)S(1)} %collective-permute-done), channel_id=1, source_target_pairs={{31,0},{0,1},{1,2},{2,3},{3,4},{4,5},{5,6},{6,7},{7,8},{8,9},{9,10... | collective-permute-start | bytes 1769480 | tf_op jit(solution)/shard_map/ppermute | solution.py:12
  34.7 24.8 %collective-permute-start.8 = (bf16[256,1152]{1,0:T(8,128)(2,1)S(1)}, bf16[256,1152]{1,0:T(8,128)(2,1)S(1)}, u32[]{:S(2)}, u32[]{:S(2)}) collective-permute-start(bf16[256,1152]{1,0:T(8,128)(2,1)S(1)} %add_convert_fusion.6), channel_id=1, source_target_pairs={{31,0},{0,1},{1,2},{2,3},{3,4},{4,5},{5,6},{6,7},{7,8},{8,9},{9,10... | collective-permute-start | bytes 1769480 | tf_op jit(solution)/shard_map/ppermute | solution.py:12
  46.9 25.3 %collective-permute-start.2 = (bf16[256,1152]{1,0:T(8,128)(2,1)S(1)}, bf16[256,1152]{1,0:T(8,128)(2,1)S(1)}, u32[]{:S(2)}, u32[]{:S(2)}) collective-permute-start(bf16[256,1152]{1,0:T(8,128)(2,1)S(1)} %collective-permute-done.1), channel_id=1, source_target_pairs={{31,0},{0,1},{1,2},{2,3},{3,4},{4,5},{5,6},{6,7},{7,8},{8,9},{9,10... | collective-permute-start | bytes 1769480 | tf_op jit(solution)/shard_map/ppermute | solution.py:12
  59.7 25.2 %collective-permute-start.9 = (bf16[256,1152]{1,0:T(8,128)(2,1)S(1)}, bf16[256,1152]{1,0:T(8,128)(2,1)S(1)}, u32[]{:S(2)}, u32[]{:S(2)}) collective-permute-start(bf16[256,1152]{1,0:T(8,128)(2,1)S(1)} %add_convert_fusion.5), channel_id=1, source_target_pairs={{31,0},{0,1},{1,2},{2,3},{3,4},{4,5},{5,6},{6,7},{7,8},{8,9},{9,10... | collective-permute-start | bytes 1769480 | tf_op jit(solution)/shard_map/ppermute | solution.py:12
  72.2 25.3 %collective-permute-start.3 = (bf16[256,1152]{1,0:T(8,128)(2,1)S(1)}, bf16[256,1152]{1,0:T(8,128)(2,1)S(1)}, u32[]{:S(2)}, u32[]{:S(2)}) collective-permute-start(bf16[256,1152]{1,0:T(8,128)(2,1)S(1)} %collective-permute-done.2), channel_id=1, source_target_pairs={{31,0},{0,1},{1,2},{2,3},{3,4},{4,5},{5,6},{6,7},{7,8},{8,9},{9,10... | collective-permute-start | bytes 1769480 | tf_op jit(solution)/shard_map/ppermute | solution.py:12
  84.9 25.2 %collective-permute-start.10 = (bf16[256,1152]{1,0:T(8,128)(2,1)S(1)}, bf16[256,1152]{1,0:T(8,128)(2,1)S(1)}, u32[]{:S(2)}, u32[]{:S(2)}) collective-permute-start(bf16[256,1152]{1,0:T(8,128)(2,1)S(1)} %add_convert_fusion.4), channel_id=1, source_target_pairs={{31,0},{0,1},{1,2},{2,3},{3,4},{4,5},{5,6},{6,7},{7,8},{8,9},{9,10... | collective-permute-start | bytes 1769480 | tf_op jit(solution)/shard_map/ppermute | solution.py:12
  97.5 25.3 %collective-permute-start.4 = (bf16[256,1152]{1,0:T(8,128)(2,1)S(1)}, bf16[256,1152]{1,0:T(8,128)(2,1)S(1)}, u32[]{:S(2)}, u32[]{:S(2)}) collective-permute-start(bf16[256,1152]{1,0:T(8,128)(2,1)S(1)} %collective-permute-done.3), channel_id=1, source_target_pairs={{31,0},{0,1},{1,2},{2,3},{3,4},{4,5},{5,6},{6,7},{7,8},{8,9},{9,10... | collective-permute-start | bytes 1769480 | tf_op jit(solution)/shard_map/ppermute | solution.py:12
  110.2 25.2 %collective-permute-start.11 = (bf16[256,1152]{1,0:T(8,128)(2,1)S(1)}, bf16[256,1152]{1,0:T(8,128)(2,1)S(1)}, u32[]{:S(2)}, u32[]{:S(2)}) collective-permute-start(bf16[256,1152]{1,0:T(8,128)(2,1)S(1)} %add_convert_fusion.3), channel_id=1, source_target_pairs={{31,0},{0,1},{1,2},{2,3},{3,4},{4,5},{5,6},{6,7},{7,8},{8,9},{9,10... | collective-permute-start | bytes 1769480 | tf_op jit(solution)/shard_map/ppermute | solution.py:12
  122.8 25.3 %collective-permute-start.5 = (bf16[256,1152]{1,0:T(8,128)(2,1)S(1)}, bf16[256,1152]{1,0:T(8,128)(2,1)S(1)}, u32[]{:S(2)}, u32[]{:S(2)}) collective-permute-start(bf16[256,1152]{1,0:T(8,128)(2,1)S(1)} %collective-permute-done.4), channel_id=1, source_target_pairs={{31,0},{0,1},{1,2},{2,3},{3,4},{4,5},{5,6},{6,7},{7,8},{8,9},{9,10... | collective-permute-start | bytes 1769480 | tf_op jit(solution)/shard_map/ppermute | solution.py:12
  135.5 25.2 %collective-permute-start.12 = (bf16[256,1152]{1,0:T(8,128)(2,1)S(1)}, bf16[256,1152]{1,0:T(8,128)(2,1)S(1)}, u32[]{:S(2)}, u32[]{:S(2)}) collective-permute-start(bf16[256,1152]{1,0:T(8,128)(2,1)S(1)} %add_convert_fusion.2), channel_id=1, source_target_pairs={{31,0},{0,1},{1,2},{2,3},{3,4},{4,5},{5,6},{6,7},{7,8},{8,9},{9,10... | collective-permute-start | bytes 1769480 | tf_op jit(solution)/shard_map/ppermute | solution.py:12
  148.0 25.3 %collective-permute-start.6 = (bf16[256,1152]{1,0:T(8,128)(2,1)S(1)}, bf16[256,1152]{1,0:T(8,128)(2,1)S(1)}, u32[]{:S(2)}, u32[]{:S(2)}) collective-permute-start(bf16[256,1152]{1,0:T(8,128)(2,1)S(1)} %collective-permute-done.5), channel_id=1, source_target_pairs={{31,0},{0,1},{1,2},{2,3},{3,4},{4,5},{5,6},{6,7},{7,8},{8,9},{9,10... | collective-permute-start | bytes 1769480 | tf_op jit(solution)/shard_map/ppermute | solution.py:12
  160.8 25.2 %collective-permute-start.13 = (bf16[256,1152]{1,0:T(8,128)(2,1)S(1)}, bf16[256,1152]{1,0:T(8,128)(2,1)S(1)}, u32[]{:S(2)}, u32[]{:S(2)}) collective-permute-start(bf16[256,1152]{1,0:T(8,128)(2,1)S(1)} %add_convert_fusion.1), channel_id=1, source_target_pairs={{31,0},{0,1},{1,2},{2,3},{3,4},{4,5},{5,6},{6,7},{7,8},{8,9},{9,10... | collective-permute-start | bytes 1769480 | tf_op jit(solution)/shard_map/ppermute | solution.py:12
  186.1 18.2 %collective-permute-start.14 = (bf16[256,1152]{1,0:T(8,128)(2,1)S(1)}, bf16[256,1152]{1,0:T(8,128)(2,1)S(1)}, u32[]{:S(2)}, u32[]{:S(2)}) collective-permute-start(bf16[256,1152]{1,0:T(8,128)(2,1)S(1)} %add_convert_fusion), channel_id=1, source_target_pairs={{7,0},{8,1},{9,2},{10,3},{11,4},{12,5},{13,6},{14,7},{15,8},{16,9}... | collective-permute-start | bytes 1769480 | tf_op jit(solution)/shard_map/ppermute | solution.py:12
  187.2 17.0 %copy-start.1 = (bf16[256,1152]{1,0:T(8,128)(2,1)S(1)}, bf16[256,1152]{1,0:T(8,128)(2,1)}, u32[]{:S(2)}) copy-start(bf16[256,1152]{1,0:T(8,128)(2,1)} %param.5) | copy-start | bytes 1769476
where the time goes:
time: 206 us
  waiting for transfers between devices  181 us (88%)
  matrix products  11.6 us (6%)
  other arithmetic  6.88 us (3%)
  starting transfers between devices  4.19 us (2%)
  between operations  2.14 us (1%)
    ppermute x15, waiting for transfers between devices, passed_along(): return lax.ppermute(block, axis, route)  181 us
    dot_general x8, matrix products, pairwise_loss_terms(): lax.dot_general(image_block_rows, text_block_rows, (((1,), (1,)), ((), ()...  4.68 us
    ppermute x15, starting transfers between devices, passed_along(): return lax.ppermute(block, axis, route)  4.19 us
  transfers between devices with their start and end apart: 15, of which 15 were waited for; matrix products, arithmetic and copies ran while one was open for 7% of the time, Pallas kernels for 0%

commit v1 on v0

--- a/solution.py
+++ b/solution.py
@@ -1,6 +1,10 @@
+import functools
+
 import jax
 import jax.numpy as jnp
 from jax import lax
+from jax.experimental import pallas as pl
+from jax.experimental.pallas import tpu as pltpu
 from jax.sharding import PartitionSpec as P
 
 KSTEPS = 8
@@ -104,9 +108,292 @@
     return (row_total_sum, grad_images, grad_texts)
 
 
+MESH = pl.DeviceIdType.MESH
+A_NEAR, B_NEAR, X_NEAR, A_FAR, B_FAR, F_FAR = range(6)
+KINDS = 6
+A_UP, A_DOWN, B_UP, B_DOWN, A_CORE, A_COLUMN, B_COLUMN, F_CORE = range(8)
+SENDS = 8
+LANES = 128
+
+
+def column_kernel(
+    columns,
+    deep,
+    scale_ref,
+    offset_ref,
+    img_ref,
+    txt_ref,
+    loss_ref,
+    grad_img_ref,
+    grad_txt_ref,
+    held,
+    total,
+    losses,
+    send_sem,
+    recv_sem,
+):
+    blk = lax.axis_index("blk")
+    z = lax.axis_index("grp")
+    core = lax.rem(blk, 2)
+    column = blk // 2
+    onward = 1 - 2 * core
+    after = lax.rem(column + onward + columns, columns)
+    before = lax.rem(column - onward + columns, columns)
+    sibling = (2 * column + 1 - core, z)
+    above, below = (blk, z + 1), (blk, z - 1)
+    after_same = (2 * after + core, z)
+    before_same = (2 * before + core, z)
+    before_other = (2 * before + 1 - core, z)
+    rows, width = img_ref.shape
+    scale, offset = scale_ref[0], offset_ref[0]
+
+    def beyond(zp):
+        return (zp - z) * onward > 0
+
+    def short(zp):
+        return (zp - z) * onward < 0
+
+    def slot(kind, zp):
+        return kind * deep + zp
+
+    def transfer(send, source, target, zp, device):
+        return pltpu.make_async_remote_copy(
+            src_ref=held.at[slot(source, zp)],
+            dst_ref=held.at[slot(target, zp)],
+            send_sem=send_sem.at[send * deep + zp],
+            recv_sem=recv_sem.at[slot(target, zp)],
+            device_id=device,
+            device_id_type=MESH,
+        )
+
+    def arrived(kind, zp):
+        transfer(A_UP, kind, kind, zp, sibling).wait_recv()
+
+    def sent(send, zp):
+        transfer(send, A_NEAR, A_NEAR, zp, sibling).wait_send()
+
+    def unit(ref):
+        raw = ref[...].astype(jnp.float32)
+        inverse = lax.rsqrt(jnp.sum(raw * raw, axis=-1, keepdims=True) + 1e-06)
+        return raw * inverse, inverse
+
+    @pl.when(core == 0)
+    def _():
+        held[slot(A_NEAR, z)] = unit(txt_ref)[0].astype(jnp.bfloat16)
+        held[slot(B_NEAR, z)] = unit(img_ref)[0].astype(jnp.bfloat16)
+
+    @pl.when(core == 1)
+    def _():
+        held[slot(A_NEAR, z)] = unit(img_ref)[0].astype(jnp.bfloat16)
+        held[slot(B_NEAR, z)] = unit(txt_ref)[0].astype(jnp.bfloat16)
+
+    barrier = pltpu.get_barrier_semaphore()
+    for device in (sibling, after_same, before_same, before_other):
+        pl.semaphore_signal(barrier, inc=1, device_id=device, device_id_type=MESH)
+
+    @pl.when(z < deep - 1)
+    def _():
+        pl.semaphore_signal(barrier, inc=1, device_id=above, device_id_type=MESH)
+
+    @pl.when(z > 0)
+    def _():
+        pl.semaphore_signal(barrier, inc=1, device_id=below, device_id_type=MESH)
+
+    total[...] = jnp.zeros_like(total)
+    losses[...] = jnp.zeros_like(losses)
+    edges = jnp.where(z > 0, 1, 0) + jnp.where(z < deep - 1, 1, 0)
+    pl.semaphore_wait(barrier, 4 + edges)
+
+    def pass_on(zp, distance):
+        def along(up, down, kind):
+            @pl.when((zp <= z) & (z < deep - 1))
+            def _():
+                transfer(up, kind, kind, zp, above).start()
+
+            @pl.when((zp >= z) & (z > 0))
+            def _():
+                transfer(down, kind, kind, zp, below).start()
+
+        @pl.when(distance > 0)
+        def _():
+            arrived(A_NEAR, zp)
+
+        along(A_UP, A_DOWN, A_NEAR)
+
+        @pl.when(beyond(zp))
+        def _():
+            transfer(A_COLUMN, A_NEAR, A_FAR, zp, after_same).start()
+
+        transfer(A_CORE, A_NEAR, X_NEAR, zp, sibling).start()
+
+        @pl.when(distance > 0)
+        def _():
+            arrived(B_NEAR, zp)
+
+        along(B_UP, B_DOWN, B_NEAR)
+        transfer(B_COLUMN, B_NEAR, B_FAR, zp, before_other).start()
+
+    diagonal = lax.broadcasted_iota(jnp.int32, (rows, rows), 0) == lax.broadcasted_iota(
+        jnp.int32, (rows, rows), 1
+    )
+
+    def meet(role, own, other, same):
+        logits = (
+            scale
+            * lax.dot_general(
+                held[own],
+                held[other],
+                (((1,), (1,)), ((), ())),
+                preferred_element_type=jnp.float32,
+            )
+            + offset
+        )
+        sign = jnp.where(diagonal & same, -1.0, 1.0)
+        turned = sign * logits
+        small = jnp.exp(-jnp.abs(turned))
+        loss = jnp.maximum(turned, 0.0) + jnp.log1p(small)
+        sigmoid = jnp.where(turned >= 0.0, 1.0, small) / (1.0 + small)
+        weights = (sign * sigmoid * scale).astype(jnp.bfloat16)
+        part = loss[:, :LANES]
+        for at in range(LANES, rows, LANES):
+            part = part + loss[:, at : at + LANES]
+        losses[role] += part
+        step = 384 if width % 384 == 0 else width
+        for at in range(0, width, step):
+            total[role, :, at : at + step] += jnp.dot(
+                weights, held[other, :, at : at + step], preferred_element_type=jnp.float32
+            )
+
+    def work(zp):
+        arrived(B_FAR, zp)
+
+        @pl.when(beyond(zp))
+        def _():
+            transfer(F_CORE, B_FAR, F_FAR, zp, sibling).start()
+            arrived(A_FAR, zp)
+
+        arrived(X_NEAR, zp)
+
+        @pl.when(short(zp))
+        def _():
+            arrived(F_FAR, zp)
+
+        def tile(which, carry):
+            role = which // 2
+            kind_p = jnp.where(beyond(zp), A_FAR, A_NEAR)
+            kind_q = jnp.where(short(zp), F_FAR, B_NEAR)
+            kind = jnp.where(
+                which == 0,
+                kind_p,
+                jnp.where(which == 1, B_FAR, jnp.where(which == 2, kind_q, X_NEAR)),
+            )
+            own = jnp.where(role == 0, slot(B_NEAR, z), slot(A_NEAR, z))
+            meet(role, own, slot(kind, zp), (lax.rem(which, 2) == 0) & (zp == z))
+            return carry
+
+        lax.fori_loop(0, 4, tile, 0)
+
+    def both_ways(distance, action):
+        @pl.when(z - distance >= 0)
+        def _():
+            action(z - distance)
+
+        @pl.when((distance > 0) & (z + distance < deep))
+        def _():
+            action(z + distance)
+
+    def turn(distance, carry):
+        @pl.when(distance < deep)
+        def _():
+            both_ways(distance, lambda zp: pass_on(zp, distance))
+
+        @pl.when(distance > 0)
+        def _():
+            @pl.when(z - distance + 1 >= 0)
+            def _():
+                work(z - distance + 1)
+
+            @pl.when((distance > 1) & (z + distance - 1 < deep))
+            def _():
+                work(z + distance - 1)
+
+        return carry
+
+    lax.fori_loop(0, deep + 1, turn, 0)
+
+    def finish(ref, role):
+        unit32, inverse = unit(ref)
+        grad = total[role]
+        along = jnp.sum(unit32 * grad, axis=-1, keepdims=True)
+        return inverse * (grad - unit32 * along)
+
+    grad_img_ref[...] = finish(img_ref, core)
+    grad_txt_ref[...] = finish(txt_ref, 1 - core)
+    loss_ref[...] = jnp.sum(losses[core], axis=-1, keepdims=True)
+
+    def settle(zp, carry):
+        @pl.when((zp <= z) & (z < deep - 1))
+        def _():
+            sent(A_UP, zp)
+            sent(B_UP, zp)
+
+        @pl.when((zp >= z) & (z > 0))
+        def _():
+            sent(A_DOWN, zp)
+            sent(B_DOWN, zp)
+
+        @pl.when(beyond(zp))
+        def _():
+            sent(A_COLUMN, zp)
+            sent(F_CORE, zp)
+
+        sent(A_CORE, zp)
+        sent(B_COLUMN, zp)
+        return carry
+
+    lax.fori_loop(0, deep, settle, 0)
+
+
+def on_column(columns, deep, images, texts, scale, offset):
+    rows, width = images.shape
+    tiles = 4 * deep
+    loss, grad_images, grad_texts = pl.pallas_call(
+        functools.partial(column_kernel, columns, deep),
+        out_shape=(
+            jax.ShapeDtypeStruct((rows, 1), jnp.float32),
+            jax.ShapeDtypeStruct((rows, width), jnp.float32),
+            jax.ShapeDtypeStruct((rows, width), jnp.float32),
+        ),
+        in_specs=[pl.BlockSpec(memory_space=pltpu.SMEM)] * 2
+        + [pl.BlockSpec(memory_space=pltpu.VMEM)] * 2,
+        out_specs=[pl.BlockSpec(memory_space=pltpu.VMEM)] * 3,
+        scratch_shapes=[
+            pltpu.VMEM((KINDS * deep, rows, width), jnp.bfloat16),
+            pltpu.VMEM((2, rows, width), jnp.float32),
+            pltpu.VMEM((2, rows, LANES), jnp.float32),
+            pltpu.SemaphoreType.DMA((SENDS * deep,)),
+            pltpu.SemaphoreType.DMA((KINDS * deep,)),
+        ],
+        compiler_params=pltpu.CompilerParams(
+            collective_id=0, has_side_effects=True, vmem_limit_bytes=48 * 1024 * 1024
+        ),
+        cost_estimate=pl.CostEstimate(
+            flops=tiles * 4 * rows * rows * width,
+            bytes_accessed=12 * rows * width,
+            transcendentals=tiles * 3 * rows * rows,
+        ),
+        name="column",
+    )(scale, offset, images, texts)
+    return loss.reshape(rows), grad_images, grad_texts
+
+
 def solution(mesh):
+    blocks, deep = mesh.shape["blk"], mesh.shape["grp"]
+    body = on_device
+    if KSTEPS == 2 * deep and blocks % 2 == 0 and blocks >= 6:
+        body = functools.partial(on_column, blocks // 2, deep)
     return jax.shard_map(
-        on_device,
+        body,
         mesh=mesh,
         in_specs=(P(("blk", "grp"), None), P(("blk", "grp"), None), P(), P()),
         out_specs=(P(("blk", "grp")), P(("blk", "grp"), None), P(("blk", "grp"), None)),

time: 206 us -> 109 us (0.53)
  waiting for transfers between devices: 181 us -> 0 us
  Pallas kernels: 0 us -> 102 us
  matrix products: 11.6 us -> 0 us
  other arithmetic: 6.88 us -> 0.68 us
  starting transfers between devices: 4.19 us -> 0 us
  local copies, waits for them, and re-layouts: 0.01 us -> 4.15 us
    ppermute x15 -> x0, waiting for transfers between devices: 181 us -> none  [passed_along(): return lax.ppermute(block, axis, route)]
    pallas_call x0 -> x1, Pallas kernels: none -> 102 us  [on_column(): pl.pallas_call(functools.partial(column_kernel, columns, deep), out_shape...]
    dot_general x24 -> x0, matrix products: 11.6 us -> none  [the longest x8 4.68 us: pairwise_loss_terms(): lax.dot_general(image_block_rows, text_block_rows, (((1,), (1,)), ((), ()...]
    ppermute x15 -> x0, starting transfers between devices: 4.19 us -> none  [passed_along(): return lax.ppermute(block, axis, route)]
    unnamed x4 -> x6, local copies, waits for them, and re-layouts: 0.01 us -> 4.15 us
    mul x2 -> x0, other arithmetic: 2.58 us -> none  [back_norm(): return inverse * (grad_unit - unit32 * along)]
  transfers between devices with their start and end apart: 15 -> 0, of which waited for: 15 -> 0; matrix products, arithmetic and copies ran while one was open for 7% -> 0% of each run, Pallas kernels for 0% -> 0%
where the time goes in v1:
time: 109 us; the launch traced here: 108 us
  Pallas kernels  102 us (94%)
  local copies, waits for them, and re-layouts  4.15 us (4%)
  between operations  1.94 us (2%)
    pallas_call x1, Pallas kernels, on_column(): pl.pallas_call(functools.partial(column_kernel, columns, deep), out_shape...  102 us
    unnamed x6, local copies, waits for them, and re-layouts  4.15 us

profile of v1, /device:TPU:1, one launch (start us, length us, event | category | flops | bytes accessed | tf_op | source)
XLA Modules:
  0.0 108.5 jit_solution(2670581848943524521)
XLA Ops:
  1.9 0.0 copy-start
  1.9 1.1 copy-done
  3.0 0.0 copy-start.1
  3.0 1.1 copy-done.1
  4.1 101.7 %column.1 = (f32[256,1]{1,0:T(8,128)S(1)}, f32[256,1152]{1,0:T(8,128)S(1)}, f32[256,1152]{1,0:T(8,128)S(1)}) custom-call(f32[1]{0:T(128)S(6)} %copy.9.scale_ref, f32[1]{0:T(128)S(6)} %copy.10.offset_ref, bf16[256,1152]{1,0:T(8,128)(2,1)S(1)} %copy-done, bf16[256,1152]{1,0:T(8,128)(2,1)S(1)} %copy-done.1), custom_call_target="tpu_custom_call" | custom-call | flops 4831838208 | bytes 3538944 | tf_op jit(solution)/shard_map/column/pallas_call | solution.py:360
  105.8 0.7 reduce
  106.5 1.0 copy.11
  107.5 1.0 copy.12
Async XLA Ops:
  1.9 1.1 copy-start
  3.0 1.1 copy-start.1
